TPU v7x, 32 devices: a whole 2x2x4 slice. The times are simulated.
32 devices in a mesh: groups: 2 (over x), expert: 8 (over z, y), dp: 2 (over core).
Axes of the slice: x: 2, y: 2, z: 4, core: 2. Of those that a mesh axis runs over, the one named last changes fastest.
Arguments:
- tokens: bfloat16 [4096, 2048], P(('groups', 'expert', 'dp')), parts along dimension 0, may hold values from -6 to 6
- expert_ids: int32 [4096, 8], P(('groups', 'expert', 'dp')), parts along dimension 0, may hold values from 0 to 31, all different within a row; in each aligned block of 128 rows (0 to 127, 128 to 255, ...) at most 40 rows name the same one
- logits: float32 [4096, 8], P(('groups', 'expert', 'dp')), parts along dimension 0
- cotangent: bfloat16 [4096, 2048], P(('groups', 'expert', 'dp')), parts along dimension 0, may hold values from -6 to 6
- w_gate: bfloat16 [32, 2048, 768], P(('expert', 'dp')), may hold values from -0.125 to 0.125
- w_up: bfloat16 [32, 2048, 768], P(('expert', 'dp')), may hold values from -0.125 to 0.125
- w_down: bfloat16 [32, 768, 2048], P(('expert', 'dp')), may hold values from -0.21875 to 0.21875
Outputs:
- mixed: bfloat16 [4096, 2048], P(('groups', 'expert', 'dp')), parts along dimension 0
- grad_tokens: bfloat16 [4096, 2048], P(('groups', 'expert', 'dp')), parts along dimension 0
- grad_logits: float32 [4096, 8], P(('groups', 'expert', 'dp')), parts along dimension 0
- grad_down: bfloat16 [64, 768, 2048], P(('groups', 'expert', 'dp')), parts along dimension 0
There are 2 independent parts, one for each index of `groups`. A program takes and returns all parts, laid end to end along the dimension named above; an argument that names none is the same for every part. Nothing has to cross between parts.
Inputs may be any that keep to these rules, and one draw needn't show every extreme that they name: `expert_ids`: each row names 8 different experts; within the rows of one device no expert is named by more than 40 rows, a bound that some block reaches.
All inputs are finite; a program needn't handle non-finite values.
Results may differ from a plain program's by a relative error of at most 0.0064.
Values may be sent and summed in bfloat16 or wider, within the bound.
A program may use at most 192 MiB of HBM per device.

v0:
```python
import jax
import jax.numpy as jnp
from jax import lax
from jax.sharding import PartitionSpec as P


def swiglu_pass(rows_in, cot_rows, weight_gate, weight_up, weight_down):
    gate_pre = jnp.einsum("erd,edf->erf", rows_in, weight_gate, preferred_element_type=jnp.float32)
    up_pre = jnp.einsum("erd,edf->erf", rows_in, weight_up, preferred_element_type=jnp.float32)
    sigmoid_gate = jax.nn.sigmoid(gate_pre)
    silu_gate = gate_pre * sigmoid_gate
    hidden = (silu_gate * up_pre).astype(jnp.bfloat16)
    expert_out = jnp.einsum(
        "erf,efd->erd", hidden, weight_down, preferred_element_type=jnp.float32
    ).astype(jnp.bfloat16)
    grad_hidden = jnp.einsum(
        "erd,efd->erf", cot_rows, weight_down, preferred_element_type=jnp.float32
    )
    grad_gate = (
        grad_hidden * up_pre * sigmoid_gate * (1.0 + gate_pre * (1.0 - sigmoid_gate))
    ).astype(jnp.bfloat16)
    grad_up = (grad_hidden * silu_gate).astype(jnp.bfloat16)
    grad_input = (
        jnp.einsum("erf,edf->erd", grad_gate, weight_gate, preferred_element_type=jnp.float32)
        + jnp.einsum("erf,edf->erd", grad_up, weight_up, preferred_element_type=jnp.float32)
    ).astype(jnp.bfloat16)
    grad_weight = jnp.einsum("erf,erd->efd", hidden, cot_rows, preferred_element_type=jnp.float32)
    return (expert_out, grad_input, grad_weight)


def on_device(tokens, expert_ids, logits, cotangent, w_gate, w_up, w_down):
    tok_rows, model_width = tokens.shape
    top_count = expert_ids.shape[1]
    local_experts = w_gate.shape[0]
    expert_devices = lax.axis_size("expert")
    pair_devices = lax.axis_size("dp")
    group_devices = expert_devices * pair_devices
    experts_all = local_experts * group_devices
    capacity = 5 * tok_rows * top_count // (4 * experts_all)
    gate_probs = jax.nn.softmax(logits, axis=-1)
    chosen = expert_ids.reshape(-1)
    choice_rows = chosen.shape[0]
    columns = jnp.arange(experts_all, dtype=jnp.int32)
    onehot = (chosen[:, None] == columns[None, :]).astype(jnp.int32)
    before = jnp.cumsum(onehot, axis=0) - onehot
    slot_rank = jnp.sum(before * onehot, axis=1)
    slot_index = chosen * capacity + slot_rank
    repeated = jnp.broadcast_to(tokens[:, None, :], (tok_rows, top_count, model_width)).reshape(
        choice_rows, model_width
    )
    scaled_cot = (gate_probs[:, :, None] * cotangent[:, None, :].astype(jnp.float32)).astype(
        jnp.bfloat16
    )
    scaled_cot = scaled_cot.reshape(choice_rows, model_width)
    payload = jnp.concatenate([repeated, scaled_cot], axis=1)
    outgoing = (
        jnp.zeros((experts_all * capacity, 2 * model_width), jnp.bfloat16)
        .at[slot_index]
        .set(payload)
    )
    parcels = outgoing.reshape(group_devices, local_experts, capacity, 2 * model_width)
    arrived = lax.all_to_all(parcels, ("expert", "dp"), split_axis=0, concat_axis=2, tiled=True)
    arrived = arrived.reshape(local_experts, group_devices * capacity, 2 * model_width)
    expert_out, grad_input, grad_weight = swiglu_pass(
        arrived[:, :, :model_width], arrived[:, :, model_width:], w_gate, w_up, w_down
    )
    grad_down = grad_weight.astype(jnp.bfloat16)
    answers = jnp.concatenate([expert_out, grad_input], axis=2)
    answers = answers.reshape(1, local_experts, group_devices * capacity, 2 * model_width)
    returned = lax.all_to_all(answers, ("expert", "dp"), split_axis=2, concat_axis=0, tiled=True)
    returned = returned.reshape(experts_all * capacity, 2 * model_width)
    picked = returned[slot_index]
    out_choice = (
        picked[:, :model_width].astype(jnp.float32).reshape(tok_rows, top_count, model_width)
    )
    input_choice = (
        picked[:, model_width:].astype(jnp.float32).reshape(tok_rows, top_count, model_width)
    )
    mixed = jnp.sum(gate_probs[:, :, None] * out_choice, axis=1).astype(jnp.bfloat16)
    grad_tokens = jnp.sum(input_choice, axis=1).astype(jnp.bfloat16)
    inner = jnp.sum(cotangent.astype(jnp.float32)[:, None, :] * out_choice, axis=-1)
    grad_logits = gate_probs * (inner - jnp.sum(gate_probs * inner, axis=-1, keepdims=True))
    return (mixed, grad_tokens, grad_logits, grad_down)


def solution(mesh):
    return jax.shard_map(
        on_device,
        mesh=mesh,
        in_specs=(
            P(("groups", "expert", "dp"), None),
            P(("groups", "expert", "dp"), None),
            P(("groups", "expert", "dp"), None),
            P(("groups", "expert", "dp"), None),
            P(("expert", "dp"), None, None),
            P(("expert", "dp"), None, None),
            P(("expert", "dp"), None, None),
        ),
        out_specs=(
            P(("groups", "expert", "dp"), None),
            P(("groups", "expert", "dp"), None),
            P(("groups", "expert", "dp"), None),
            P(("groups", "expert", "dp"), None, None),
        ),
        check_vma=False,
    )
```

profile of v0, /device:TPU:13, one launch (start us, length us, event | category | flops | bytes accessed | tf_op | source)
XLA Modules:
  0.0 680.6 jit_solution(10669525265945229121)
XLA Ops:
  0.6 0.0 copy-start
  0.6 0.7 broadcast_multiply_fusion
  1.4 0.8 copy.39
  2.2 0.1 eq.29
  2.3 0.1 eq.25
  2.4 0.7 reduce_max.9
  3.1 0.7 fusion.28
  3.8 0.7 fusion.27
  4.5 0.1 copy.37
  4.6 0.1 mul.84
  4.7 0.1 copy.38
  4.8 0.1 mul.82
  4.9 9.0 %reduce-window.6 = s32[32,8,128]{2,1,0:T(8,128)S(1)} reduce-window(s32[32,8,128]{2,1,0:T(8,128)S(1)} %fusion.26, s32[]{:T(128)} %constant.4.clone.1), window={size=1x1x128 pad=0_0x0_0x127_0}, to_apply=%region_2.0 | reduce-window | flops 4161536 | bytes 262148 | tf_op jit(solution)/shard_map/reduce-window
  13.9 0.1 slice.26
  14.0 0.1 copy.41
  14.2 0.1 copy.42
  14.3 0.1 broadcast_add_fusion
  14.4 1.1 convert_element_type.46
  15.5 0.0 copy-done
  15.5 0.7 broadcast_bitcast_fusion
  16.2 2.5 fusion.2
  18.7 6.7 pad.3
  25.4 4.2 pad.2
  29.6 21.1 %scatter_custom_fusion = bf16[1280,4096]{1,0:T(8,128)(2,1)} fusion(s32[1024]{0:T(1024)S(1)} %bitcast.69, bf16[1024,4096]{1,0:T(8,128)(2,1)} %pad.2, bf16[1024,4096]{1,0:T(8,128)(2,1)} %pad.3, bf16[]{:T(256)} %constant.9.clone.1), kind=kCustom, calls=%fused_computation.11 | custom fusion | flops 4194304 | bytes 27262978 | tf_op jit(solution)/shard_map/scatter | solution.py:59
  50.7 233.7 %all_to_all.30 = bf16[16,2,40,4096]{3,2,1,0:T(8,128)(2,1)} all-to-all(bf16[16,2,40,4096]{3,2,1,0:T(8,128)(2,1)} %bitcast.60), channel_id=1, replica_groups=mesh['groups'=2,'expert'=8,'dp'=2] {'expert','dp'}, dimensions={0} | all-to-all | bytes 20971520 | tf_op jit(solution)/shard_map/all_to_all | solution.py:62
  284.4 9.6 %copy.44 = bf16[1,2,16,40,4096]{4,3,2,1,0:T(8,128)(2,1)} copy(bf16[1,2,16,40,4096]{4,3,1,2,0:T(8,128)(2,1)} %bitcast.61) | data formatting | bytes 20971520 | tf_op jit(solution)/shard_map/all_to_all | solution.py:62
  294.0 0.0 copy-start.3
  294.0 8.1 %fusion.13 = f32[2,640,768]{2,1,0:T(8,128)S(1)} fusion(bf16[2,2048,768]{2,1,0:T(8,128)(2,1)} %param.11, bf16[2,640,4096]{2,1,0:T(8,128)(2,1)} %bitcast.62), kind=kOutput, calls=%fused_computation.20 | convolution fusion | flops 4026531840 | bytes 15466496 | tf_op jit(solution)/shard_map/erd,edf->erf/dot_general | solution.py:8
  302.2 0.0 copy-done.3
  302.2 0.0 copy-start.5
  302.2 10.6 %fusion.9 = f32[2,640,768]{2,1,0:T(8,128)} fusion(bf16[2,768,2048]{2,1,0:T(8,128)(2,1)} %param.13, bf16[2,640,4096]{2,1,0:T(8,128)(2,1)S(1)} %bitcast.64), kind=kOutput, calls=%fused_computation.16 | convolution fusion | flops 4026531840 | bytes 15466496 | tf_op jit(solution)/shard_map/erd,efd->erf/dot_general | solution.py:16
  312.8 0.0 copy-done.5
  312.8 9.2 %multiply_convert_fusion.2 = (bf16[2,640,768]{2,1,0:T(8,128)(2,1)S(1)}, f32[2,640,768]{2,1,0:T(8,128)}) fusion(f32[2,640,768]{2,1,0:T(8,128)S(1)} %fusion.13, bf16[2,2048,768]{2,1,0:T(8,128)(2,1)} %param.12, bf16[2,640,4096]{2,1,0:T(8,128)(2,1)S(1)} %bitcast.65), kind=kOutput, calls=%fused_computation.28 | convolution fusion | flops 4032430080 | bytes 21364736 | tf_op jit(solution)/shard_map/erd,edf->erf/dot_general | solution.py:9
  322.0 0.0 copy-start.6
  322.0 9.7 %convolution_convert_fusion = bf16[2,640,2048]{2,1,0:T(8,128)(2,1)} fusion(bf16[2,640,768]{2,1,0:T(8,128)(2,1)S(1)} %get-tuple-element.12, bf16[2,768,2048]{2,1,0:T(8,128)(2,1)} %param.13), kind=kOutput, calls=%fused_computation.25 | convolution fusion | flops 4029153280 | bytes 13500416 | tf_op jit(solution)/shard_map/erf,efd->erd/dot_general | solution.py:13
  331.6 0.0 copy-done.6
  331.7 15.2 %fusion.20 = f32[2,640,2048]{2,1,0:T(8,128)} fusion(bf16[2,2048,768]{2,1,0:T(8,128)(2,1)} %param.11, f32[2,640,768]{2,1,0:T(8,128)} %copy-done.5, f32[2,640,768]{2,1,0:T(8,128)} %fusion.9, f32[2,640,768]{2,1,0:T(8,128)} %get-tuple-element.13), kind=kOutput, calls=%fused_computation.32 | convolution fusion | flops 4036362240 | bytes 28573696 | tf_op jit(solution)/shard_map/erf,edf->erd/dot_general | solution.py:24
  346.9 14.8 %add_convert_fusion = bf16[2,640,2048]{2,1,0:T(8,128)(2,1)} fusion(f32[2,640,2048]{2,1,0:T(8,128)} %fusion.20, bf16[2,2048,768]{2,1,0:T(8,128)(2,1)} %param.12, f32[2,640,768]{2,1,0:T(8,128)} %fusion.9, f32[2,640,768]{2,1,0:T(8,128)} %copy-done.5), kind=kOutput, calls=%fused_computation.6 | convolution fusion | flops 4037672960 | bytes 29884416 | tf_op jit(solution)/shard_map/erf,edf->erd/dot_general | solution.py:25
  361.7 5.6 maximum_bitcast_fusion
  367.3 27.7 %copy.45 = bf16[1,2,640,4096]{3,1,0,2:T(2,128)(2,1)} copy(bf16[1,2,640,4096]{3,2,1,0:T(8,128)(2,1)S(1)} %maximum_bitcast_fusion) | data formatting | bytes 20971520 | tf_op jit(solution)/shard_map/reshape | solution.py:69
  395.0 6.3 all-to-all-start.1
  401.3 9.8 %fusion.15 = bf16[2,768,2048]{2,1,0:T(8,128)(2,1)} fusion(bf16[2,640,768]{2,1,0:T(8,128)(2,1)} %copy-done.6, bf16[2,640,4096]{2,1,0:T(8,128)(2,1)} %bitcast.63), kind=kOutput, calls=%fused_computation.22 | convolution fusion | flops 4029677568 | bytes 13500416 | tf_op jit(solution)/shard_map/erf,erd->efd/dot_general | solution.py:27
  411.0 217.4 %all-to-all-done.1 = bf16[1,2,640,4096]{3,1,0,2:T(2,128)(2,1)} async-done(((bf16[1,2,640,4096]{3,1,0,2:T(2,128)(2,1)}), bf16[1,2,640,4096]{3,1,0,2:T(2,128)(2,1)}, u32[]{:S(2)}, u32[]{:S(2)}) %all-to-all-start.1) | async-done | bytes 10485792 | tf_op jit(solution)/shard_map/all_to_all | solution.py:70
  628.4 15.6 %copy.46 = bf16[1,2,16,40,4096]{4,3,1,2,0:T(8,128)(2,1)} copy(bf16[1,2,16,40,4096]{4,1,3,2,0:T(2,128)(2,1)} %bitcast.11) | data formatting | bytes 20971520 | tf_op jit(solution)/shard_map/all_to_all | solution.py:70
  644.0 0.0 copy-start.1
  644.0 20.8 %gather_fusion = bf16[1024,4096]{1,0:T(8,128)(2,1)} fusion(bf16[1280,4096]{1,0:T(8,128)(2,1)} %bitcast.59, s32[1024]{0:T(1024)S(1)} %broadcast_clamp_fusion), kind=kCustom, calls=%fused_computation | custom fusion | bytes 16781312 | tf_op jit(solution)/shard_map/gather | solution.py:72
  664.7 0.0 copy-start.2
  664.7 0.0 copy-start.4
  664.7 2.9 fusion.3
  667.6 8.0 %fusion.1 = bf16[128,2048]{1,0:T(8,128)(2,1)} fusion(f32[128,8]{1,0:T(8,128)S(1)} %copy.37, bf16[1024,4096]{1,0:T(8,128)(2,1)} %gather_fusion), kind=kLoop, calls=%fused_computation.8 | loop fusion | flops 6029312 | bytes 4722688 | tf_op jit(solution)/shard_map/reduce_sum | solution.py:79
  675.6 0.0 copy-done.2
  675.6 3.7 fusion.18
  679.3 0.1 reduce_sum.64
  679.5 0.0 copy-done.4
  679.5 0.6 subtract_multiply_fusion
  680.1 0.0 copy-done.1
  (8 shorter events, 0.2 us)
Async XLA Ops:
  0.6 14.9 %copy-start = (bf16[128,2048]{1,0:T(8,128)(2,1)S(1)}, bf16[128,2048]{1,0:T(8,128)(2,1)}, u32[]{:S(2)}) copy-start(bf16[128,2048]{1,0:T(8,128)(2,1)} %param.7) | copy-start | bytes 1572868
  294.0 8.2 %copy-start.3 = (bf16[1,2,16,40,4096]{4,3,2,1,0:T(8,128)(2,1)S(1)}, bf16[1,2,16,40,4096]{4,3,2,1,0:T(8,128)(2,1)}, u32[]{:S(2)}) copy-start(bf16[1,2,16,40,4096]{4,3,2,1,0:T(8,128)(2,1)} %copy.44) | copy-start | bytes 31457284
  302.2 10.6 %copy-start.5 = (f32[2,640,768]{2,1,0:T(8,128)}, f32[2,640,768]{2,1,0:T(8,128)S(1)}, u32[]{:S(2)}) copy-start(f32[2,640,768]{2,1,0:T(8,128)S(1)} %fusion.13) | copy-start | bytes 11796484
  322.0 9.7 %copy-start.6 = (bf16[2,640,768]{2,1,0:T(8,128)(2,1)}, bf16[2,640,768]{2,1,0:T(8,128)(2,1)S(1)}, u32[]{:S(2)}) copy-start(bf16[2,640,768]{2,1,0:T(8,128)(2,1)S(1)} %get-tuple-element.12) | copy-start | bytes 5898244
  395.0 233.4 %all-to-all-start.1 = ((bf16[1,2,640,4096]{3,1,0,2:T(2,128)(2,1)}), bf16[1,2,640,4096]{3,1,0,2:T(2,128)(2,1)}, u32[]{:S(2)}, u32[]{:S(2)}) async-start(bf16[1,2,640,4096]{3,1,0,2:T(2,128)(2,1)} %copy.45), calls=%async_computation.1 | async-start | bytes 20971520 | tf_op jit(solution)/shard_map/all_to_all | solution.py:70
  644.0 36.2 %copy-start.1 = (bf16[128,2048]{1,0:T(8,128)(2,1)S(1)}, bf16[128,2048]{1,0:T(8,128)(2,1)}, u32[]{:S(2)}) copy-start(bf16[128,2048]{1,0:T(8,128)(2,1)} %param.7) | copy-start | bytes 1572868
  664.7 10.9 %copy-start.2 = (bf16[1024,4096]{1,0:T(8,128)(2,1)S(1)}, bf16[1024,4096]{1,0:T(8,128)(2,1)}, u32[]{:S(2)}) copy-start(bf16[1024,4096]{1,0:T(8,128)(2,1)} %gather_fusion) | copy-start | bytes 25165828
  664.7 14.7 %copy-start.4 = (f32[128,8]{0,1:T(8,128)S(1)}, f32[128,8]{0,1:T(8,128)}, u32[]{:S(2)}) copy-start(f32[128,8]{0,1:T(8,128)} %param.9) | copy-start | bytes 12292
where the time goes:
time: 689 us; the launch traced here: 681 us
  blocking collectives  234 us (34%)
  waiting for transfers between devices  217 us (31%)
  local copies, waits for them, and re-layouts  87 us (13%)
  matrix products  77.4 us (11%)
  other arithmetic  57.6 us (8%)
    all_to_all x1, blocking collectives, on_device(): lax.all_to_all(parcels, ('expert', 'dp'), split_axis=0, concat_axis=2, ti...  234 us
    all_to_all x1, waiting for transfers between devices, on_device(): lax.all_to_all(answers, ('expert', 'dp'), split_axis=2, concat_axis=0, ti...  217 us
    reshape x1, local copies, waits for them, and re-layouts, on_device(): answers.reshape(1, local_experts, group_devices * capacity, 2 * model_width)  27.7 us
    scatter x1, other arithmetic, on_device(): outgoing = jnp.zeros((experts_all * capacity, 2 * model_width), jnp.bfloa...  21.1 us
    gather x1, local copies, waits for them, and re-layouts, on_device(): picked = returned[slot_index]  20.8 us
    all_to_all x1, local copies, waits for them, and re-layouts, on_device(): lax.all_to_all(answers, ('expert', 'dp'), split_axis=2, concat_axis=0, ti...  15.6 us
    dot_general x1, matrix products, swiglu_pass(): jnp.einsum('erf,edf->erd', grad_gate, weight_gate, preferred_element_type...  15.2 us
    dot_general x1, matrix products, swiglu_pass(): jnp.einsum('erf,edf->erd', grad_up, weight_up, preferred_element_type=jnp...  14.8 us
  transfers between devices with their start and end apart: 1, of which 1 were waited for; matrix products, arithmetic and copies ran while one was open for 1% of the time, Pallas kernels for 0%

commit v1 on v0

v1 whole, which is shorter than its diff:
```python
import functools

import jax
import jax.numpy as jnp
from jax import lax
from jax.experimental import pallas as pl
from jax.experimental.pallas import tpu as pltpu
from jax.sharding import PartitionSpec as P

BF16 = jnp.bfloat16
F32 = jnp.float32
LAST = (((1,), (1,)), ((), ()))
FIRST = (((0,), (0,)), ((), ()))
VMEM_LIMIT = 60 * 1024 * 1024


def dot(a, b, dims=(((1,), (0,)), ((), ()))):
    return lax.dot_general(a, b, dims, preferred_element_type=F32)


def one_hot(pos_ref, e, b, rows):
    pos = pos_ref[e, b]
    return lax.broadcasted_iota(jnp.int32, (rows, pos.shape[1]), 0) == pos


def gather_rows(e, all_ref, pos_ref, dest_ref, rows, in_buf, in_sem):
    blocks, span = pos_ref.shape[1], pos_ref.shape[3]

    def fetch(b):
        slot = lax.rem(b, 2)
        source = all_ref.at[pl.ds(pl.multiple_of(b * span, span), span), :]
        return pltpu.make_async_copy(source, in_buf.at[slot], in_sem.at[slot])

    fetch(jnp.int32(0)).start()

    def step(b, carry):
        @pl.when(b + 1 < blocks)
        def _():
            fetch(b + 1).start()

        fetch(b).wait()
        pick = one_hot(pos_ref, e, b, rows).astype(BF16)
        chosen = dot(pick, in_buf[lax.rem(b, 2)]).astype(BF16)
        dest_ref[pl.ds(pl.multiple_of(b * rows, 16), rows), :] = chosen
        return carry

    lax.fori_loop(0, blocks, step, 0)


def scatter_rows(pos_ref, rows_ref, out_ref, rows, out_buf, out_sem):
    experts, blocks, span = pos_ref.shape[0], pos_ref.shape[1], pos_ref.shape[3]

    def send(b):
        slot = lax.rem(b, 2)
        target = out_ref.at[pl.ds(pl.multiple_of(b * span, span), span), :]
        return pltpu.make_async_copy(out_buf.at[slot], target, out_sem.at[slot])

    def step(b, carry):
        @pl.when(b >= 2)
        def _():
            send(b - 2).wait()

        here = pl.ds(pl.multiple_of(b * rows, 16), rows)
        total = None
        for e in range(experts):
            pick = one_hot(pos_ref, e, b, rows).astype(BF16)
            part = dot(pick, rows_ref[e, here, :], FIRST)
            total = part if total is None else total + part
        out_buf[lax.rem(b, 2)] = total.astype(BF16)
        send(b).start()
        return carry

    lax.fori_loop(0, blocks, step, 0)
    for b in range(max(0, blocks - 2), blocks):
        send(jnp.int32(b)).wait()


def forward_kernel(rows, tok_ref, pos_ref, p_ref, wg_ref, wu_ref, wd_ref,
                   g_ref, u_ref, prow_ref, hp_ref, mix_ref, x_ref, o_ref,
                   in_buf, out_buf, in_sem, out_sem):
    e = pl.program_id(0)
    blocks = pos_ref.shape[1]
    width, ff = wg_ref.shape[1], wg_ref.shape[2]
    gather_rows(e, tok_ref, pos_ref, x_ref, rows, in_buf, in_sem)

    def weigh(b, carry):
        pick = one_hot(pos_ref, e, b, rows)
        prob = jnp.sum(jnp.where(pick, p_ref[e, b], 0.0), axis=1, keepdims=True)
        prow_ref[0, pl.ds(pl.multiple_of(b * rows, 16), rows), :] = jnp.broadcast_to(prob, (rows, 128))
        return carry

    lax.fori_loop(0, blocks, weigh, 0)
    prob = prow_ref[0, :, 0:1]
    tile = 256
    for f in range(ff // tile):
        cols = slice(f * tile, (f + 1) * tile)
        gate = dot(x_ref[...], wg_ref[0, :, cols])
        up = dot(x_ref[...], wu_ref[0, :, cols])
        g_ref[0, :, cols] = gate
        u_ref[0, :, cols] = up
        hidden = gate * jax.nn.sigmoid(gate) * up
        hp_ref[0, :, cols] = (prob * hidden).astype(BF16)

    def outputs(n, carry):
        cols = pl.ds(pl.multiple_of(n * 256, 256), 256)
        o_ref[e, :, cols] = dot(hp_ref[0], wd_ref[0, :, cols]).astype(BF16)
        return carry

    lax.fori_loop(0, width // 256, outputs, 0)

    @pl.when(e == pl.num_programs(0) - 1)
    def _():
        scatter_rows(pos_ref, o_ref, mix_ref, rows, out_buf, out_sem)


def backward_kernel(rows, all_experts, me_ref, cot_ref, pos_ref, g_ref, u_ref, prow_ref, wg_ref,
                    wu_ref, wd_ref, crow_ref, gt_ref, gg_ref, gu_ref, gi_ref,
                    in_buf, out_buf, in_sem, out_sem):
    e = pl.program_id(0)
    width, ff = wg_ref.shape[1], wg_ref.shape[2]
    gather_rows(e, cot_ref, pos_ref, crow_ref.at[0], rows, in_buf, in_sem)
    prob = prow_ref[0, :, 0:1]
    inner = jnp.zeros_like(prob)
    tile = 256
    for f in range(ff // tile):
        cols = slice(f * tile, (f + 1) * tile)
        raw = dot(crow_ref[0], wd_ref[0, cols, :], LAST)
        gate = g_ref[0, :, cols]
        up = u_ref[0, :, cols]
        sig = jax.nn.sigmoid(gate)
        silu = gate * sig
        inner = inner + jnp.sum(raw * (silu * up), axis=1, keepdims=True)
        grad = prob * raw
        gg_ref[:, cols] = (grad * up * sig * (1.0 + gate * (1.0 - sig))).astype(BF16)
        gu_ref[:, cols] = (grad * silu).astype(BF16)

    def inputs(n, carry):
        cols = pl.ds(pl.multiple_of(n * 256, 256), 256)
        total = dot(gg_ref[...], wg_ref[0, cols, :], LAST) + dot(gu_ref[...], wu_ref[0, cols, :], LAST)
        gi_ref[e, :, cols] = total.astype(BF16)
        return carry

    lax.fori_loop(0, width // 256, inputs, 0)
    extra = gi_ref.shape[2] - width
    high = inner.astype(BF16).astype(F32)
    low = inner - high
    lane = lax.broadcasted_iota(jnp.int32, (inner.shape[0], extra), 1)
    mine = me_ref[0] * pl.num_programs(0) + e
    packed = jnp.where(lane == mine, high, jnp.where(lane == mine + all_experts, low, 0.0))
    gi_ref[e, :, width:] = packed.astype(BF16)

    @pl.when(e == pl.num_programs(0) - 1)
    def _():
        scatter_rows(pos_ref, gi_ref, gt_ref, rows, out_buf, out_sem)


def whole(shape):
    return pl.BlockSpec(shape, lambda e: (0,) * len(shape), pipeline_mode=pl.Buffered(1))


def by_expert(shape):
    return pl.BlockSpec((1,) + shape[1:], lambda e: (e,) + (0,) * (len(shape) - 1))


def on_device(tokens, expert_ids, logits, cotangent, w_gate, w_up, w_down):
    axes = ("expert", "dp")
    tok_rows, width = tokens.shape
    top = expert_ids.shape[1]
    local, _, ff = w_gate.shape
    devices = lax.axis_size("expert") * lax.axis_size("dp")
    experts = local * devices
    capacity = 5 * tok_rows * top // (4 * experts)
    fold = max(1, 80 // capacity)
    rows, span, blocks = fold * capacity, fold * tok_rows, devices // fold
    all_rows = rows * blocks
    me = lax.axis_index(axes)

    every_tok = lax.all_gather(tokens, axes, axis=0, tiled=True)
    every_cot = lax.all_gather(cotangent, axes, axis=0, tiled=True)

    probs = jax.nn.softmax(logits, axis=-1)
    chosen = expert_ids[:, :, None] == jnp.arange(experts, dtype=jnp.int32)
    named = jnp.any(chosen, axis=1)
    dense = jnp.sum(jnp.where(chosen, probs[:, :, None], 0.0), axis=1)
    before = jnp.tril(jnp.ones((tok_rows, tok_rows), BF16), -1)
    rank = dot(before, named.astype(BF16))
    place = jnp.where(named, rank, -1000.0)
    small = lax.all_gather(jnp.concatenate([dense.T, place.T], axis=0), axes, axis=0, tiled=False)
    own_p = lax.dynamic_slice_in_dim(small, me * local, local, axis=1)
    own_pos = lax.dynamic_slice_in_dim(small, experts + me * local, local, axis=1)
    shift = (jnp.arange(devices) % fold * capacity).astype(F32)
    own_pos = (own_pos + shift[:, None, None]).astype(jnp.int32)
    own_p = own_p.transpose(1, 0, 2).reshape(local, blocks, 1, span)
    own_pos = own_pos.transpose(1, 0, 2).reshape(local, blocks, 1, span)

    params = pltpu.CompilerParams(vmem_limit_bytes=VMEM_LIMIT, dimension_semantics=("arbitrary",))
    unit = 2 * local * all_rows * width * ff
    f_shape, w_shape = (local, all_rows, ff), (local, width, ff)
    gate, up, prow, hp, mix = pl.pallas_call(
        functools.partial(forward_kernel, rows),
        grid=(local,),
        in_specs=[pl.BlockSpec(memory_space=pl.ANY), whole(own_pos.shape), whole(own_p.shape),
                  by_expert(w_gate.shape), by_expert(w_up.shape), by_expert(w_down.shape)],
        out_specs=[by_expert(f_shape), by_expert(f_shape), by_expert((local, all_rows, 128)),
                   by_expert(f_shape), pl.BlockSpec(memory_space=pl.ANY)],
        out_shape=[jax.ShapeDtypeStruct(f_shape, F32), jax.ShapeDtypeStruct(f_shape, F32),
                   jax.ShapeDtypeStruct((local, all_rows, 128), F32),
                   jax.ShapeDtypeStruct(f_shape, BF16),
                   jax.ShapeDtypeStruct((devices * tok_rows, width), BF16)],
        scratch_shapes=[pltpu.VMEM((all_rows, width), BF16),
                        pltpu.VMEM((local, all_rows, width), BF16),
                        pltpu.VMEM((2, span, width), BF16), pltpu.VMEM((2, span, width), BF16),
                        pltpu.SemaphoreType.DMA((2,)), pltpu.SemaphoreType.DMA((2,))],
        compiler_params=params,
        cost_estimate=pl.CostEstimate(flops=3 * unit, bytes_accessed=40 << 20, transcendentals=0),
        name="forward",
    )(every_tok, own_pos, own_p, w_gate, w_up, w_down)
    mixed = lax.psum_scatter(mix, axes, scatter_dimension=0, tiled=True)

    extra = -(-2 * experts // 128) * 128
    crow, gt = pl.pallas_call(
        functools.partial(backward_kernel, rows, experts),
        grid=(local,),
        in_specs=[pl.BlockSpec(memory_space=pltpu.SMEM), pl.BlockSpec(memory_space=pl.ANY), whole(own_pos.shape),
                  by_expert(f_shape), by_expert(f_shape), by_expert((local, all_rows, 128)),
                  by_expert(w_gate.shape), by_expert(w_up.shape), by_expert(w_down.shape)],
        out_specs=[by_expert((local, all_rows, width)), pl.BlockSpec(memory_space=pl.ANY)],
        out_shape=[jax.ShapeDtypeStruct((local, all_rows, width), BF16),
                   jax.ShapeDtypeStruct((devices * tok_rows, width + extra), BF16)],
        scratch_shapes=[pltpu.VMEM((all_rows, ff), BF16), pltpu.VMEM((all_rows, ff), BF16),
                        pltpu.VMEM((local, all_rows, width + extra), BF16),
                        pltpu.VMEM((2, span, width), BF16), pltpu.VMEM((2, span, width + extra), BF16),
                        pltpu.SemaphoreType.DMA((2,)), pltpu.SemaphoreType.DMA((2,))],
        compiler_params=params,
        cost_estimate=pl.CostEstimate(flops=3 * unit, bytes_accessed=40 << 20, transcendentals=0),
        name="backward",
    )(me.reshape(1).astype(jnp.int32), every_cot, own_pos, gate, up, prow, w_gate, w_up, w_down)
    gt, mixed = lax.optimization_barrier((gt, mixed))
    summed = lax.psum_scatter(gt, axes, scatter_dimension=0, tiled=True)

    grad_down = jnp.einsum("erf,erd->efd", hp, crow, preferred_element_type=F32).astype(BF16)
    grad_tokens = summed[:, :width]
    tail = summed[:, width:].astype(F32)
    products = tail[:, :experts] + tail[:, experts : 2 * experts]
    inner = jnp.sum(jnp.where(chosen, products[:, None, :], 0.0), axis=-1)
    grad_logits = probs * (inner - jnp.sum(probs * inner, axis=-1, keepdims=True))
    return (mixed, grad_tokens, grad_logits, grad_down)


def solution(mesh):
    rows = P(("groups", "expert", "dp"), None)
    weights = P(("expert", "dp"), None, None)
    return jax.shard_map(
        on_device,
        mesh=mesh,
        in_specs=(rows, rows, rows, rows, weights, weights, weights),
        out_specs=(rows, rows, rows, P(("groups", "expert", "dp"), None, None)),
        check_vma=False,
    )
```

time: 689 us -> 395 us (0.57)
  blocking collectives: 234 us -> 18.2 us
  Pallas kernels: 0 us -> 97.6 us
  local copies, waits for them, and re-layouts: 87 us -> 2.58 us
  matrix products: 77.4 us -> 9.71 us
  other arithmetic: 57.6 us -> 5.75 us
  waiting for transfers between devices: 217 us -> 245 us
  between operations: 1.25 us -> 13.9 us
    all_to_all x1 -> x0, blocking collectives: 234 us -> none  [on_device(): lax.all_to_all(parcels, ('expert', 'dp'), split_axis=0, concat_axis=2, ti...]
    all_to_all x1 -> x0, waiting for transfers between devices: 217 us -> none  [on_device(): lax.all_to_all(answers, ('expert', 'dp'), split_axis=2, concat_axis=0, ti...]
    reduce_scatter x0 -> x2, waiting for transfers between devices: none -> 161 us  [the longest x1 102 us: on_device(): summed = lax.psum_scatter(gt, axes, scatter_dimension=0, tiled=True)]
    pallas_call x0 -> x2, Pallas kernels: none -> 97.6 us  [the longest x1 49.9 us: on_device(): pl.pallas_call(functools.partial(backward_kernel, rows, experts), grid=(l...]
    all_gather x0 -> x2, waiting for transfers between devices: none -> 82.4 us  [the longest x1 54.9 us: on_device(): every_tok = lax.all_gather(tokens, axes, axis=0, tiled=True)]
    dot_general x7 -> x2, matrix products: 77.4 us -> 9.71 us  [the longest x1 9.51 us: on_device(): jnp.einsum('erf,erd->efd', hp, crow, preferred_element_type=F32)]
    reshape x2 -> x0, local copies, waits for them, and re-layouts: 28.3 us -> none  [the longest x1 27.7 us: on_device(): answers.reshape(1, local_experts, group_devices * capacity, 2 * model_width)]
    all_to_all x2 -> x0, local copies, waits for them, and re-layouts: 25.2 us -> none  [the longest x1 15.6 us: on_device(): lax.all_to_all(answers, ('expert', 'dp'), split_axis=2, concat_axis=0, ti...]
  transfers between devices with their start and end apart: 1 -> 4, of which waited for: 1 -> 4; matrix products, arithmetic and copies ran while one was open for 1% -> 4% of each run, Pallas kernels for 0% -> 25%
where the time goes in v1:
time: 395 us; the launch traced here: 392 us
  waiting for transfers between devices  245 us (62%)
  Pallas kernels  97.6 us (25%)
  blocking collectives  18.2 us (5%)
  between operations  13.9 us (4%)
  matrix products  9.71 us (2%)
  other arithmetic  5.75 us (1%)
    reduce_scatter x1, waiting for transfers between devices, on_device(): summed = lax.psum_scatter(gt, axes, scatter_dimension=0, tiled=True)  102 us
    reduce_scatter x1, waiting for transfers between devices, on_device(): mixed = lax.psum_scatter(mix, axes, scatter_dimension=0, tiled=True)  58.8 us
    all_gather x1, waiting for transfers between devices, on_device(): every_tok = lax.all_gather(tokens, axes, axis=0, tiled=True)  54.9 us
    pallas_call x1, Pallas kernels, on_device(): pl.pallas_call(functools.partial(backward_kernel, rows, experts), grid=(l...  49.9 us
    pallas_call x1, Pallas kernels, on_device(): pl.pallas_call(functools.partial(forward_kernel, rows), grid=(local,), in...  47.8 us
    all_gather x1, waiting for transfers between devices, on_device(): every_cot = lax.all_gather(cotangent, axes, axis=0, tiled=True)  27.5 us
    all_gather x1, blocking collectives, on_device(): lax.all_gather(jnp.concatenate([dense.T, place.T], axis=0), axes, axis=0,...  18.2 us
    dot_general x1, matrix products, on_device(): jnp.einsum('erf,erd->efd', hp, crow, preferred_element_type=F32)  9.51 us
  transfers between devices with their start and end apart: 4, of which 4 were waited for; matrix products, arithmetic and copies ran while one was open for 4% of the time, Pallas kernels for 25%

profile of v1, /device:TPU:13, one launch (start us, length us, event | category | flops | bytes accessed | tf_op | source)
XLA Modules:
  0.0 392.4 jit_solution(15519397385060717890)
XLA Ops:
  7.2 0.0 all-gather.6.cloned.1.call-start
  7.2 0.7 all-gather.6.cloned.1.call-update
  7.9 0.0 all-gather.4.cloned.1.call-start
  7.9 0.7 all-gather.4.cloned.1.call-update
  8.6 0.0 reduce-scatter.3.cloned.1.call-start
  8.7 0.7 reduce_max.9
  9.4 0.7 fusion.8
  10.1 0.7 fusion
  10.8 0.7 fusion.7
  11.5 0.7 select_reduce_fusion.1
  12.2 0.2 convolution_select_fusion
  12.4 18.2 %all-gather = f32[1024,128]{1,0:T(8,128)S(1)} all-gather(f32[64,128]{1,0:T(8,128)S(1)} %pad_maximum_fusion), channel_id=2, replica_groups=mesh['groups'=2,'expert'=8,'dp'=2] {'expert','dp'}, dimensions={0}, use_global_device_ids=true | all-gather | bytes 557056 | tf_op jit(solution)/shard_map/all_gather | solution.py:188
  30.7 0.6 copy.22
  31.3 0.7 fusion.4
  32.0 54.9 %all-gather.6.cloned.1.call-done.tok_ref = bf16[2048,2048]{1,0:T(8,128)(2,1)} async-done(((bf16[128,2048]{1,0:T(8,128)(2,1)}), bf16[2048,2048]{1,0:T(8,128)(2,1)}) %all-gather.6.cloned.1.call-update) | async-done | bytes 8388624 | tf_op jit(solution)/shard_map/all_gather | solution.py:178
  86.9 47.8 %forward.1 = (f32[2,640,768]{2,1,0:T(8,128)}, f32[2,640,768]{2,1,0:T(8,128)}, f32[2,640,128]{2,1,0:T(8,128)}, bf16[2,640,768]{2,1,0:T(8,128)(2,1)}, bf16[2048,2048]{1,0:T(8,128)(2,1)}) custom-call(bf16[2048,2048]{1,0:T(8,128)(2,1)} %all-gather.6.cloned.1.call-done.tok_ref, s32[2,8,1,256]{3,2,1,0:T(1,128)} %bitcast.16, f32[2,8,1,256]{3,2,1,0:T(1,128)} %bitcast.18, ...), custom_call_target="tpu_custom_call" | custom-call | flops 12079595520 | bytes 41943040 | tf_op jit(solution)/shard_map/forward/pallas_call | solution.py:199
  134.6 0.0 reduce-scatter.3.cloned.1.call-update
  134.7 0.0 reduce-scatter.5.cloned.1.call-start
  134.7 27.5 %all-gather.4.cloned.1.call-done.cot_ref = bf16[2048,2048]{1,0:T(8,128)(2,1)} async-done(((bf16[128,2048]{1,0:T(8,128)(2,1)}), bf16[2048,2048]{1,0:T(8,128)(2,1)}) %all-gather.4.cloned.1.call-update) | async-done | bytes 8388624 | tf_op jit(solution)/shard_map/all_gather | solution.py:179
  162.2 49.9 %backward.1 = (bf16[2,640,2048]{2,1,0:T(8,128)(2,1)}, bf16[2048,2176]{1,0:T(8,128)(2,1)}) custom-call(s32[1]{0:T(128)} %bitcast.me_ref, bf16[2048,2048]{1,0:T(8,128)(2,1)} %all-gather.4.cloned.1.call-done.cot_ref, s32[2,8,1,256]{3,2,1,0:T(1,128)} %bitcast.17, f32[2,640,768]{2,1,0:T(8,128)} %get-tuple-element.13.g_ref, ...), custom_call_target="tpu_custom_call" | custom-call | flops 12079595520 | bytes 41943040 | tf_op jit(solution)/shard_map/backward/pallas_call | solution.py:221
  212.1 0.0 copy-start.2
  212.1 58.8 %reduce-scatter.3.cloned.1.call-done = bf16[128,2048]{1,0:T(8,128)(2,1)} async-done(((bf16[2048,2048]{1,0:T(8,128)(2,1)}), bf16[128,2048]{1,0:T(8,128)(2,1)}) %reduce-scatter.3.cloned.1.call-update) | async-done | bytes 524304 | tf_op jit(solution)/shard_map/reduce_scatter | solution.py:218
  270.9 0.0 reduce-scatter.5.cloned.1.call-update
  270.9 0.0 copy-done.2
  270.9 0.0 copy-start.1
  270.9 0.0 copy-start
  270.9 9.5 %convolution_convert_fusion = bf16[2,768,2048]{2,1,0:T(8,128)(2,1)} fusion(bf16[2,640,768]{2,1,0:T(8,128)(2,1)S(1)} %copy-done.2, bf16[2,640,2048]{2,1,0:T(8,128)(2,1)} %get-tuple-element.21), kind=kOutput, calls=%fused_computation | convolution fusion | flops 4029677568 | bytes 13500416 | tf_op jit(solution)/shard_map/erf,erd->efd/dot_general | solution.py:241
  280.5 101.9 %reduce-scatter.5.cloned.1.call-done = bf16[128,2176]{1,0:T(8,128)(2,1)} async-done(((bf16[2048,2176]{1,0:T(8,128)(2,1)}), bf16[128,2176]{1,0:T(8,128)(2,1)}) %reduce-scatter.5.cloned.1.call-update) | async-done | bytes 557072 | tf_op jit(solution)/shard_map/reduce_scatter | solution.py:239
  382.4 0.8 slice_convert_fusion
  383.1 0.1 slice_add_fusion
  383.2 0.1 copy.18
  383.3 0.0 copy-done.1
  383.3 0.0 copy-done
  383.4 0.6 subtract_multiply_fusion
  384.0 1.9 slice.16
  (6 shorter events, 0.1 us)
Async XLA Ops:
  7.2 79.7 %all-gather.6.cloned.1.call-start = ((), (), s32[]{:S(2)}) async-start(), calls=%async_computation.3 | async-start | bytes 8912896 | tf_op jit(solution)/shard_map/all_gather | solution.py:178
  7.9 154.3 %all-gather.4.cloned.1.call-start = ((), (), s32[]{:S(2)}) async-start(), calls=%async_computation.2 | async-start | bytes 8912896 | tf_op jit(solution)/shard_map/all_gather | solution.py:179
  8.6 262.2 %reduce-scatter.3.cloned.1.call-start = ((), (), s32[]{:S(2)}) async-start(), calls=%async_computation.4 | async-start | bytes 8912896 | tf_op jit(solution)/shard_map/reduce_scatter | solution.py:218
  134.7 247.7 %reduce-scatter.5.cloned.1.call-start = ((), (), s32[]{:S(2)}) async-start(), calls=%async_computation.5 | async-start | bytes 9469952 | tf_op jit(solution)/shard_map/reduce_scatter | solution.py:239
  212.1 58.8 %copy-start.2 = (bf16[2,640,768]{2,1,0:T(8,128)(2,1)S(1)}, bf16[2,640,768]{2,1,0:T(8,128)(2,1)}, u32[]{:S(2)}) copy-start(bf16[2,640,768]{2,1,0:T(8,128)(2,1)} %get-tuple-element.20) | copy-start | bytes 5898244
  270.9 112.4 %copy-start.1 = (s32[128,8]{0,1:T(8,128)S(1)}, s32[128,8]{0,1:T(8,128)}, u32[]{:S(2)}) copy-start(s32[128,8]{0,1:T(8,128)} %param.8) | copy-start | bytes 12292
  270.9 112.4 %copy-start = (f32[128,8]{0,1:T(8,128)S(1)}, f32[128,8]{0,1:T(8,128)}, u32[]{:S(2)}) copy-start(f32[128,8]{0,1:T(8,128)} %param.9) | copy-start | bytes 12292
Sparse Core Ops, SparseCore 0:
  10.2 76.6 all-gather.5
  89.0 73.1 all-gather.3
  166.9 103.9 reduce-scatter.2
  274.8 107.4 reduce-scatter.4

commit v2 on v1

--- a/solution.py
+++ b/solution.py
@@ -162,6 +162,179 @@
     return pl.BlockSpec((1,) + shape[1:], lambda e: (e,) + (0,) * (len(shape) - 1))
 
 
+def ring_place(index, n):
+    odd = index % 2
+    return (1 - odd) * (index // 2) + odd * (n - 1 - index // 2)
+
+
+def ring_index(place, n):
+    place = (place + 2 * n) % n
+    back = place // (n // 2)
+    return (1 - back) * (2 * place) + back * (2 * (n - 1 - place) + 1)
+
+
+def ring_hops(n):
+    return [(d, c, n // 2 - (d != c)) for c in range(2) for d in range(2)]
+
+
+def ring_setup(n):
+    me, side = lax.axis_index("expert"), lax.axis_index("dp")
+    place = ring_place(me, n)
+    ahead = [{"expert": ring_index(place + 1, n)}, {"expert": ring_index(place - 1, n)}]
+    sibling = {"dp": 1 - side}
+    barrier = pltpu.get_barrier_semaphore()
+    for other in ahead + [sibling]:
+        pl.semaphore_signal(barrier, inc=1, device_id=other, device_id_type=pl.DeviceIdType.MESH)
+    pl.semaphore_wait(barrier, 3)
+    return me, side, place, ahead, sibling
+
+
+def remote(source, target, send_sem, recv_sem, device):
+    return pltpu.make_async_remote_copy(
+        src_ref=source, dst_ref=target, send_sem=send_sem, recv_sem=recv_sem,
+        device_id=device, device_id_type=pl.DeviceIdType.MESH)
+
+
+def ring_gather_kernel(n, x_ref, out_ref, own_sem, send_sem, recv_sem, give_sem, take_sem, pair_sem):
+    me, side, place, ahead, sibling = ring_setup(n)
+    size = x_ref.shape[0]
+    part = size // 2
+    steps = [1, -1]
+
+    def area(dp, index, c):
+        start = pl.multiple_of((dp * n + index) * size + c * part, part)
+        return out_ref.at[pl.ds(start, part), :]
+
+    mine = out_ref.at[pl.ds(pl.multiple_of((side * n + me) * size, size), size), :]
+    other = out_ref.at[pl.ds(pl.multiple_of(((1 - side) * n + me) * size, size), size), :]
+    started = []
+    chains = ring_hops(n)
+    for d, c, hops in chains:
+        copy = remote(x_ref.at[c * part : (c + 1) * part, :], area(side, me, c),
+                      send_sem.at[d, c, 0], recv_sem.at[d, c, 0], ahead[d])
+        copy.start()
+        started.append(copy)
+    local = pltpu.make_async_copy(x_ref, mine, own_sem)
+    local.start()
+    copy = remote(x_ref, mine, pair_sem.at[0], pair_sem.at[1], sibling)
+    copy.start()
+    started.append(copy)
+    for s in range(n // 2):
+        for d, c, hops in chains:
+            if s >= hops:
+                continue
+            here = area(side, ring_index(place - steps[d] * (s + 1), n), c)
+            remote(here, here, send_sem.at[d, c, s], recv_sem.at[d, c, s], ahead[d]).wait_recv()
+            if s + 1 < hops:
+                copy = remote(here, here, send_sem.at[d, c, s + 1], recv_sem.at[d, c, s + 1], ahead[d])
+                copy.start()
+                started.append(copy)
+            copy = remote(here, here, give_sem.at[d, c, s], take_sem.at[d, c, s], sibling)
+            copy.start()
+            started.append(copy)
+    for d, c, hops in chains:
+        for s in range(hops):
+            here = area(1 - side, ring_index(place - steps[d] * (s + 1), n), c)
+            remote(here, here, give_sem.at[d, c, s], take_sem.at[d, c, s], sibling).wait_recv()
+    remote(x_ref, other, pair_sem.at[0], pair_sem.at[1], sibling).wait_recv()
+    for copy in started:
+        copy.wait_send()
+    local.wait()
+
+
+def ring_gather(block):
+    n = lax.axis_size("expert")
+    size, width = block.shape
+    sems = pltpu.SemaphoreType.DMA((2, 2, n // 2))
+    return pl.pallas_call(
+        functools.partial(ring_gather_kernel, n),
+        in_specs=[pl.BlockSpec(memory_space=pl.ANY)],
+        out_specs=pl.BlockSpec(memory_space=pl.ANY),
+        out_shape=jax.ShapeDtypeStruct((2 * n * size, width), block.dtype),
+        scratch_shapes=[pltpu.SemaphoreType.DMA, sems, sems, sems, sems, pltpu.SemaphoreType.DMA((2,))],
+        compiler_params=pltpu.CompilerParams(collective_id=0, has_side_effects=True),
+        name="ring_gather",
+    )(block)
+
+
+def ring_scatter_kernel(n, parts_ref, out_ref, sib_ref, load_ref, land_ref,
+                        give_sem, take_sem, send_sem, recv_sem):
+    me, side, place, ahead, sibling = ring_setup(n)
+    size = out_ref.shape[0]
+    part = size // 2
+    steps = [1, -1]
+    chains = ring_hops(n)
+
+    def rows(dp, off, c, count):
+        start = (dp * n + ring_index(place + off, n)) * size + c * part
+        return pl.ds(pl.multiple_of(start, part), count)
+
+    started = []
+    offsets = [n // 2]
+    for k in range(n // 2 - 1, 0, -1):
+        offsets += [k, n - k]
+    offsets.append(0)
+    for off in offsets:
+        copy = remote(parts_ref.at[rows(1 - side, off, 0, size), :], sib_ref.at[off],
+                      give_sem.at[off], take_sem.at[off], sibling)
+        copy.start()
+        started.append(copy)
+    ready = set()
+
+    def own(off, c):
+        off = off % n
+        if off not in ready:
+            ready.add(off)
+            remote(sib_ref.at[off], sib_ref.at[off], give_sem.at[off], take_sem.at[off], sibling).wait_recv()
+        return (parts_ref[rows(side, off, c, part), :].astype(F32)
+                + sib_ref[off, c * part : (c + 1) * part, :].astype(F32))
+
+    def arrived(d, c, s):
+        slot = land_ref.at[d, c, s]
+        remote(slot, slot, send_sem.at[d, c, s], recv_sem.at[d, c, s], ahead[d]).wait_recv()
+        return land_ref[d, c, s].astype(F32)
+
+    for s in range(n // 2):
+        for d, c, hops in chains:
+            if s >= hops:
+                continue
+            total = own(steps[d] * (hops - s), c)
+            if s > 0:
+                total = total + arrived(d, c, s - 1)
+            load_ref[d, c, s] = total.astype(load_ref.dtype)
+            copy = remote(load_ref.at[d, c, s], land_ref.at[d, c, s],
+                          send_sem.at[d, c, s], recv_sem.at[d, c, s], ahead[d])
+            copy.start()
+            started.append(copy)
+    for c in range(2):
+        total = own(0, c)
+        for d, half, hops in chains:
+            if half == c:
+                total = total + arrived(d, c, hops - 1)
+        out_ref[c * part : (c + 1) * part, :] = total.astype(out_ref.dtype)
+    for copy in started:
+        copy.wait_send()
+
+
+def ring_scatter(parts):
+    n = lax.axis_size("expert")
+    all_rows, width = parts.shape
+    size = all_rows // (2 * n)
+    sems = pltpu.SemaphoreType.DMA((2, 2, n // 2))
+    slots = pltpu.VMEM((2, 2, n // 2, size // 2, width), parts.dtype)
+    return pl.pallas_call(
+        functools.partial(ring_scatter_kernel, n),
+        in_specs=[pl.BlockSpec(memory_space=pltpu.VMEM)],
+        out_specs=pl.BlockSpec(memory_space=pltpu.VMEM),
+        out_shape=jax.ShapeDtypeStruct((size, width), parts.dtype),
+        scratch_shapes=[pltpu.VMEM((n, size, width), parts.dtype), slots, slots,
+                        pltpu.SemaphoreType.DMA((n,)), pltpu.SemaphoreType.DMA((n,)), sems, sems],
+        compiler_params=pltpu.CompilerParams(
+            collective_id=1, has_side_effects=True, vmem_limit_bytes=VMEM_LIMIT),
+        name="ring_scatter",
+    )(parts)
+
+
 def on_device(tokens, expert_ids, logits, cotangent, w_gate, w_up, w_down):
     axes = ("expert", "dp")
     tok_rows, width = tokens.shape
@@ -175,8 +348,7 @@
     all_rows = rows * blocks
     me = lax.axis_index(axes)
 
-    every_tok = lax.all_gather(tokens, axes, axis=0, tiled=True)
-    every_cot = lax.all_gather(cotangent, axes, axis=0, tiled=True)
+    every_cot = lax.all_gather(cotangent, ("dp", "expert"), axis=0, tiled=True)
 
     probs = jax.nn.softmax(logits, axis=-1)
     chosen = expert_ids[:, :, None] == jnp.arange(experts, dtype=jnp.int32)
@@ -185,7 +357,9 @@
     before = jnp.tril(jnp.ones((tok_rows, tok_rows), BF16), -1)
     rank = dot(before, named.astype(BF16))
     place = jnp.where(named, rank, -1000.0)
-    small = lax.all_gather(jnp.concatenate([dense.T, place.T], axis=0), axes, axis=0, tiled=False)
+    small = lax.all_gather(jnp.concatenate([dense.T, place.T], axis=0), ("dp", "expert"), axis=0, tiled=False)
+    tokens, small = lax.optimization_barrier((tokens, small))
+    every_tok = ring_gather(tokens)
     own_p = lax.dynamic_slice_in_dim(small, me * local, local, axis=1)
     own_pos = lax.dynamic_slice_in_dim(small, experts + me * local, local, axis=1)
     shift = (jnp.arange(devices) % fold * capacity).astype(F32)
@@ -215,7 +389,7 @@
         cost_estimate=pl.CostEstimate(flops=3 * unit, bytes_accessed=40 << 20, transcendentals=0),
         name="forward",
     )(every_tok, own_pos, own_p, w_gate, w_up, w_down)
-    mixed = lax.psum_scatter(mix, axes, scatter_dimension=0, tiled=True)
+    mixed = lax.psum_scatter(mix, ("dp", "expert"), scatter_dimension=0, tiled=True)
 
     extra = -(-2 * experts // 128) * 128
     crow, gt = pl.pallas_call(
@@ -235,8 +409,7 @@
         cost_estimate=pl.CostEstimate(flops=3 * unit, bytes_accessed=40 << 20, transcendentals=0),
         name="backward",
     )(me.reshape(1).astype(jnp.int32), every_cot, own_pos, gate, up, prow, w_gate, w_up, w_down)
-    gt, mixed = lax.optimization_barrier((gt, mixed))
-    summed = lax.psum_scatter(gt, axes, scatter_dimension=0, tiled=True)
+    summed = ring_scatter(gt)
 
     grad_down = jnp.einsum("erf,erd->efd", hp, crow, preferred_element_type=F32).astype(BF16)
     grad_tokens = summed[:, :width]

time: 395 us -> 326 us (0.83)
  waiting for transfers between devices: 245 us -> 0.72 us
  Pallas kernels: 97.6 us -> 258 us
  blocking collectives: 18.2 us -> 32.8 us
    reduce_scatter x2 -> x1, waiting for transfers between devices: 161 us -> 0.01 us  [on_device(): lax.psum_scatter(mix, ('dp', 'expert'), scatter_dimension=0, tiled=True)]
    pallas_call x0 -> x2, Pallas kernels: none -> 160 us  [the longest x1 83.4 us: ring_gather(): pl.pallas_call(functools.partial(ring_gather_kernel, n), in_specs=[pl.Blo...]
    all_gather x2 -> x1, waiting for transfers between devices: 82.4 us -> 0.02 us  [on_device(): every_cot = lax.all_gather(cotangent, ('dp', 'expert'), axis=0, tiled=True)]
    all_gather x1, blocking collectives: 18.2 us -> 32.8 us  [on_device(): lax.all_gather(jnp.concatenate([dense.T, place.T], axis=0), ('dp', 'exper...]
  transfers between devices with their start and end apart: 4 -> 2, of which waited for: 4 -> 0; matrix products, arithmetic and copies ran while one was open for 4% -> 5% of each run, Pallas kernels for 25% -> 80%
where the time goes in v2:
time: 326 us; the launch traced here: 324 us
  Pallas kernels  258 us (79%)
  blocking collectives  32.8 us (10%)
  between operations  14.2 us (4%)
  matrix products  9.69 us (3%)
  other arithmetic  5.75 us (2%)
    pallas_call x1, Pallas kernels, ring_gather(): pl.pallas_call(functools.partial(ring_gather_kernel, n), in_specs=[pl.Blo...  83.4 us
    pallas_call x1, Pallas kernels, ring_scatter(): pl.pallas_call(functools.partial(ring_scatter_kernel, n), in_specs=[pl.Bl...  77 us
    pallas_call x1, Pallas kernels, on_device(): pl.pallas_call(functools.partial(backward_kernel, rows, experts), grid=(l...  50.6 us
    pallas_call x1, Pallas kernels, on_device(): pl.pallas_call(functools.partial(forward_kernel, rows), grid=(local,), in...  47.5 us
    all_gather x1, blocking collectives, on_device(): lax.all_gather(jnp.concatenate([dense.T, place.T], axis=0), ('dp', 'exper...  32.8 us
    dot_general x1, matrix products, on_device(): jnp.einsum('erf,erd->efd', hp, crow, preferred_element_type=F32)  9.49 us
  transfers between devices with their start and end apart: 2, of which 0 were waited for; matrix products, arithmetic and copies ran while one was open for 5% of the time, Pallas kernels for 80%

profile of v2, /device:TPU:13, one launch (start us, length us, event | category | flops | bytes accessed | tf_op | source)
XLA Modules:
  0.0 323.9 jit_solution(90677442882365319)
XLA Ops:
  7.2 0.0 all-gather.3.cloned.1.call-start
  7.2 0.7 all-gather.3.cloned.1.call-update
  7.9 0.0 reduce-scatter.2.cloned.1.call-start
  7.9 0.7 reduce_max.9
  8.7 0.7 fusion.7
  9.4 0.7 fusion
  10.1 0.7 fusion.6
  10.8 0.7 select_reduce_fusion.1
  11.5 0.2 convolution_select_fusion
  11.7 32.8 %all-gather = f32[1024,128]{1,0:T(8,128)S(1)} all-gather(f32[64,128]{1,0:T(8,128)S(1)} %pad_maximum_fusion), channel_id=2, replica_groups=mesh['groups'=2,'expert'=8,'dp'=2] {'dp','expert'}, dimensions={0}, use_global_device_ids=true | all-gather | bytes 557056 | tf_op jit(solution)/shard_map/all_gather | solution.py:360
  44.5 83.4 %ring_gather.1.tok_ref = bf16[2048,2048]{1,0:T(8,128)(2,1)} custom-call(bf16[128,2048]{1,0:T(8,128)(2,1)} %x_ref), custom_call_target="tpu_custom_call" | custom-call | tf_op jit(solution)/shard_map/ring_gather/pallas_call | solution.py:249
  127.9 0.3 copy.16
  128.2 0.7 constant_dynamic-slice_fusion
  128.9 47.5 %forward.1 = (f32[2,640,768]{2,1,0:T(8,128)}, f32[2,640,768]{2,1,0:T(8,128)}, f32[2,640,128]{2,1,0:T(8,128)}, bf16[2,640,768]{2,1,0:T(8,128)(2,1)}, bf16[2048,2048]{1,0:T(8,128)(2,1)}) custom-call(bf16[2048,2048]{1,0:T(8,128)(2,1)} %ring_gather.1.tok_ref, s32[2,8,1,256]{3,2,1,0:T(1,128)} %bitcast.16, f32[2,8,1,256]{3,2,1,0:T(1,128)} %bitcast.18, ...), custom_call_target="tpu_custom_call" | custom-call | flops 12079595520 | bytes 41943040 | tf_op jit(solution)/shard_map/forward/pallas_call | solution.py:373
  176.4 0.0 reduce-scatter.2.cloned.1.call-update
  176.4 0.0 all-gather.3.cloned.1.call-done.cot_ref
  176.5 50.6 %backward.1 = (bf16[2,640,2048]{2,1,0:T(8,128)(2,1)}, bf16[2048,2176]{1,0:T(8,128)(2,1)}) custom-call(s32[1]{0:T(128)} %bitcast.7.me_ref, bf16[2048,2048]{1,0:T(8,128)(2,1)} %all-gather.3.cloned.1.call-done.cot_ref, s32[2,8,1,256]{3,2,1,0:T(1,128)} %bitcast.17, f32[2,640,768]{2,1,0:T(8,128)} %get-tuple-element.16.g_ref, ...), custom_call_target="tpu_custom_call" | custom-call | flops 12079595520 | bytes 41943040 | tf_op jit(solution)/shard_map/backward/pallas_call | solution.py:395
  227.1 0.0 copy-start.1
  227.1 0.0 copy-start
  227.1 0.0 copy-start.2
  227.1 77.0 %ring_scatter.1 = bf16[128,2176]{1,0:T(8,128)(2,1)} custom-call(bf16[2048,2176]{1,0:T(8,128)(2,1)} %get-tuple-element.19.parts_ref), custom_call_target="tpu_custom_call" | custom-call | tf_op jit(solution)/shard_map/ring_scatter/pallas_call | solution.py:325
  304.1 1.9 slice.12
  306.0 0.8 slice_convert_fusion
  306.8 0.1 slice_add_fusion
  306.8 0.1 copy.18
  306.9 0.0 copy-done.1
  307.0 0.0 copy-done
  307.0 0.6 subtract_multiply_fusion
  307.6 0.0 copy-done.2
  307.6 9.5 %convolution_convert_fusion = bf16[2,768,2048]{2,1,0:T(8,128)(2,1)} fusion(bf16[2,640,768]{2,1,0:T(8,128)(2,1)S(1)} %copy-done.2, bf16[2,640,2048]{2,1,0:T(8,128)(2,1)} %get-tuple-element.21), kind=kOutput, calls=%fused_computation | convolution fusion | flops 4029677568 | bytes 13500416 | tf_op jit(solution)/shard_map/erf,erd->efd/dot_general | solution.py:414
  317.1 0.0 reduce-scatter.2.cloned.1.call-done
  (5 shorter events, 0.1 us)
Async XLA Ops:
  7.2 169.3 %all-gather.3.cloned.1.call-start = ((), (), s32[]{:S(2)}) async-start(), calls=%async_computation.2 | async-start | bytes 8912896 | tf_op jit(solution)/shard_map/all_gather | solution.py:351
  7.9 309.2 %reduce-scatter.2.cloned.1.call-start = ((), (), s32[]{:S(2)}) async-start(), calls=%async_computation.1 | async-start | bytes 8912896 | tf_op jit(solution)/shard_map/reduce_scatter | solution.py:392
  227.1 79.8 %copy-start.1 = (s32[128,8]{0,1:T(8,128)S(1)}, s32[128,8]{0,1:T(8,128)}, u32[]{:S(2)}) copy-start(s32[128,8]{0,1:T(8,128)} %param.8) | copy-start | bytes 12292
  227.1 79.9 %copy-start = (f32[128,8]{0,1:T(8,128)S(1)}, f32[128,8]{0,1:T(8,128)}, u32[]{:S(2)}) copy-start(f32[128,8]{0,1:T(8,128)} %param.9) | copy-start | bytes 12292
  227.1 80.5 %copy-start.2 = (bf16[2,640,768]{2,1,0:T(8,128)(2,1)S(1)}, bf16[2,640,768]{2,1,0:T(8,128)(2,1)}, u32[]{:S(2)}) copy-start(bf16[2,640,768]{2,1,0:T(8,128)(2,1)} %get-tuple-element.20) | copy-start | bytes 5898244
Sparse Core Ops, SparseCore 0:
  10.2 107.4 all-gather.2
  176.5 127.3 reduce-scatter.1

commit v3 on v2

--- a/solution.py
+++ b/solution.py
@@ -28,7 +28,7 @@
 
     def fetch(b):
         slot = lax.rem(b, 2)
-        source = all_ref.at[pl.ds(pl.multiple_of(b * span, span), span), :]
+        source = all_ref.at[pl.ds(pl.multiple_of(b * span, span), span), 0 : in_buf.shape[2]]
         return pltpu.make_async_copy(source, in_buf.at[slot], in_sem.at[slot])
 
     fetch(jnp.int32(0)).start()
@@ -357,15 +357,15 @@
     before = jnp.tril(jnp.ones((tok_rows, tok_rows), BF16), -1)
     rank = dot(before, named.astype(BF16))
     place = jnp.where(named, rank, -1000.0)
-    small = lax.all_gather(jnp.concatenate([dense.T, place.T], axis=0), ("dp", "expert"), axis=0, tiled=False)
-    tokens, small = lax.optimization_barrier((tokens, small))
-    every_tok = ring_gather(tokens)
-    own_p = lax.dynamic_slice_in_dim(small, me * local, local, axis=1)
-    own_pos = lax.dynamic_slice_in_dim(small, experts + me * local, local, axis=1)
-    shift = (jnp.arange(devices) % fold * capacity).astype(F32)
-    own_pos = (own_pos + shift[:, None, None]).astype(jnp.int32)
-    own_p = own_p.transpose(1, 0, 2).reshape(local, blocks, 1, span)
-    own_pos = own_pos.transpose(1, 0, 2).reshape(local, blocks, 1, span)
+    high = lax.reduce_precision(dense, 8, 7)
+    notes = jnp.concatenate([high, dense - high, place], axis=1)
+    notes = jnp.pad(notes, ((0, 0), (0, -3 * experts % 128))).astype(BF16)
+    every_tok = ring_gather(jnp.concatenate([tokens, notes], axis=1))
+    tail = every_tok[:, width:].astype(F32)
+    own = [lax.dynamic_slice_in_dim(tail, k * experts + me * local, local, axis=1) for k in range(3)]
+    shift = (jnp.arange(devices * tok_rows) // tok_rows % fold * capacity).astype(F32)
+    own_p = (own[0] + own[1]).T.reshape(local, blocks, 1, span)
+    own_pos = (own[2] + shift[:, None]).astype(jnp.int32).T.reshape(local, blocks, 1, span)
 
     params = pltpu.CompilerParams(vmem_limit_bytes=VMEM_LIMIT, dimension_semantics=("arbitrary",))
     unit = 2 * local * all_rows * width * ff

time: 326 us -> 309 us (0.948)
  blocking collectives: 32.8 us -> 0 us
  Pallas kernels: 258 us -> 268 us
  other arithmetic: 5.75 us -> 9.37 us
    all_gather x1 -> x0, blocking collectives: 32.8 us -> none  [on_device(): lax.all_gather(jnp.concatenate([dense.T, place.T], axis=0), ('dp', 'exper...]
    pallas_call x1, Pallas kernels: 83.4 us -> 93.4 us  [ring_gather(): pl.pallas_call(functools.partial(ring_gather_kernel, n), in_specs=[pl.Blo...]
  transfers between devices with their start and end apart: 2 -> 2, of which waited for: 0 -> 0; matrix products, arithmetic and copies ran while one was open for 5% -> 8% of each run, Pallas kernels for 80% -> 88%
where the time goes in v3:
time: 309 us; the launch traced here: 306 us
  Pallas kernels  268 us (87%)
  between operations  14.2 us (5%)
  matrix products  9.69 us (3%)
  other arithmetic  9.37 us (3%)
  local copies, waits for them, and re-layouts  4.12 us (1%)
    pallas_call x1, Pallas kernels, ring_gather(): pl.pallas_call(functools.partial(ring_gather_kernel, n), in_specs=[pl.Blo...  93.4 us
    pallas_call x1, Pallas kernels, ring_scatter(): pl.pallas_call(functools.partial(ring_scatter_kernel, n), in_specs=[pl.Bl...  76.2 us
    pallas_call x1, Pallas kernels, on_device(): pl.pallas_call(functools.partial(backward_kernel, rows, experts), grid=(l...  50.8 us
    pallas_call x1, Pallas kernels, on_device(): pl.pallas_call(functools.partial(forward_kernel, rows), grid=(local,), in...  47.5 us
    dot_general x1, matrix products, on_device(): jnp.einsum('erf,erd->efd', hp, crow, preferred_element_type=F32)  9.49 us
  transfers between devices with their start and end apart: 2, of which 0 were waited for; matrix products, arithmetic and copies ran while one was open for 8% of the time, Pallas kernels for 88%

profile of v3, /device:TPU:13, one launch (start us, length us, event | category | flops | bytes accessed | tf_op | source)
XLA Modules:
  0.0 306.1 jit_solution(12133604999832847937)
XLA Ops:
  7.2 0.0 all-gather.2.cloned.1.call-start
  7.2 0.7 all-gather.2.cloned.1.call-update
  7.9 0.0 reduce-scatter.2.cloned.1.call-start
  7.9 0.7 reduce_max.9
  8.6 0.7 fusion.19
  9.4 0.7 fusion.18
  10.1 0.7 select_reduce_fusion.1
  10.8 0.1 copy.26
  10.9 0.7 fusion.1
  11.6 0.1 copy.28
  11.7 0.1 copy.25
  11.8 0.2 fusion
  12.0 0.1 fusion.8
  12.1 1.9 pad_maximum_fusion.x_ref
  14.0 93.4 %ring_gather.1.tok_ref = bf16[2048,2176]{1,0:T(8,128)(2,1)} custom-call(bf16[128,2176]{1,0:T(8,128)(2,1)} %pad_maximum_fusion.x_ref), custom_call_target="tpu_custom_call" | custom-call | tf_op jit(solution)/shard_map/ring_gather/pallas_call | solution.py:249
  107.4 1.1 slice_convert_fusion
  108.6 1.2 dynamic-slice_add_fusion
  109.7 0.9 copy.36.pos_ref
  110.7 0.9 copy.37.p_ref
  111.6 47.5 %forward.1 = (f32[2,640,768]{2,1,0:T(8,128)}, f32[2,640,768]{2,1,0:T(8,128)}, f32[2,640,128]{2,1,0:T(8,128)}, bf16[2,640,768]{2,1,0:T(8,128)(2,1)}, bf16[2048,2048]{1,0:T(8,128)(2,1)}) custom-call(bf16[2048,2176]{1,0:T(8,128)(2,1)} %ring_gather.1.tok_ref, s32[2,8,1,256]{3,2,1,0:T(1,128)} %copy.36.pos_ref, f32[2,8,1,256]{3,2,1,0:T(1,128)} %copy.37.p_ref, ...), custom_call_target="tpu_custom_call" | custom-call | flops 12079595520 | bytes 41943040 | tf_op jit(solution)/shard_map/forward/pallas_call | solution.py:373
  159.1 0.0 reduce-scatter.2.cloned.1.call-update
  159.1 0.0 all-gather.2.cloned.1.call-done.cot_ref
  159.1 50.8 %backward.1 = (bf16[2,640,2048]{2,1,0:T(8,128)(2,1)}, bf16[2048,2176]{1,0:T(8,128)(2,1)}) custom-call(s32[1]{0:T(128)} %bitcast.4.me_ref, bf16[2048,2048]{1,0:T(8,128)(2,1)} %all-gather.2.cloned.1.call-done.cot_ref, s32[2,8,1,256]{3,2,1,0:T(1,128)} %copy.36.pos_ref, f32[2,640,768]{2,1,0:T(8,128)} %get-tuple-element.12.g_ref, ...), custom_call_target="tpu_custom_call" | custom-call | flops 12079595520 | bytes 41943040 | tf_op jit(solution)/shard_map/backward/pallas_call | solution.py:395
  210.0 0.0 copy-start.1
  210.0 0.0 copy-start
  210.0 0.0 copy-start.2
  210.0 76.2 %ring_scatter.1 = bf16[128,2176]{1,0:T(8,128)(2,1)} custom-call(bf16[2048,2176]{1,0:T(8,128)(2,1)} %get-tuple-element.15.parts_ref), custom_call_target="tpu_custom_call" | custom-call | tf_op jit(solution)/shard_map/ring_scatter/pallas_call | solution.py:325
  286.2 1.9 slice.16
  288.1 0.8 slice_convert_fusion.1
  288.9 0.1 slice_add_fusion
  289.0 0.1 copy.32
  289.0 0.0 copy-done.1
  289.1 0.0 copy-done
  289.1 0.6 subtract_multiply_fusion
  289.7 0.0 copy-done.2
  289.7 9.5 %convolution_convert_fusion = bf16[2,768,2048]{2,1,0:T(8,128)(2,1)} fusion(bf16[2,640,768]{2,1,0:T(8,128)(2,1)S(1)} %copy-done.2, bf16[2,640,2048]{2,1,0:T(8,128)(2,1)} %get-tuple-element.17), kind=kOutput, calls=%fused_computation | convolution fusion | flops 4029677568 | bytes 13500416 | tf_op jit(solution)/shard_map/erf,erd->efd/dot_general | solution.py:414
  299.2 0.0 reduce-scatter.2.cloned.1.call-done
  (6 shorter events, 0.1 us)
Async XLA Ops:
  7.2 152.0 %all-gather.2.cloned.1.call-start = ((), (), s32[]{:S(2)}) async-start(), calls=%async_computation.2 | async-start | bytes 8912896 | tf_op jit(solution)/shard_map/all_gather | solution.py:351
  7.9 291.3 %reduce-scatter.2.cloned.1.call-start = ((), (), s32[]{:S(2)}) async-start(), calls=%async_computation.1 | async-start | bytes 8912896 | tf_op jit(solution)/shard_map/reduce_scatter | solution.py:392
  210.0 79.1 %copy-start.1 = (s32[128,8]{0,1:T(8,128)S(1)}, s32[128,8]{0,1:T(8,128)}, u32[]{:S(2)}) copy-start(s32[128,8]{0,1:T(8,128)} %param.8) | copy-start | bytes 12292
  210.0 79.1 %copy-start = (f32[128,8]{0,1:T(8,128)S(1)}, f32[128,8]{0,1:T(8,128)}, u32[]{:S(2)}) copy-start(f32[128,8]{0,1:T(8,128)} %param.9) | copy-start | bytes 12292
  210.0 79.7 %copy-start.2 = (bf16[2,640,768]{2,1,0:T(8,128)(2,1)S(1)}, bf16[2,640,768]{2,1,0:T(8,128)(2,1)}, u32[]{:S(2)}) copy-start(bf16[2,640,768]{2,1,0:T(8,128)(2,1)} %get-tuple-element.16) | copy-start | bytes 5898244
Sparse Core Ops, SparseCore 0:
  10.2 101.6 all-gather.1
  159.2 127.1 reduce-scatter.1
